TPU v7x, 32 devices: a whole 2x2x4 slice. The times are simulated.
32 devices in a mesh: wide: 8 (over z, y), narrow: 4 (over x, core).
Axes of the slice: x: 2, y: 2, z: 4, core: 2. Of those that a mesh axis runs over, the one named last changes fastest.
Arguments:
- velocity: float32 [3, 512, 4096], P(None, None, ('wide', 'narrow')), may hold values from -6 to 6
- element_slot: int32 [32, 128], P(('wide', 'narrow')), may hold values from 0 to 127, as said below
- corner_vertex: int32 [8, 4096], P(None, ('wide', 'narrow')), may hold values from 0 to 4351, as said below
- axial_size: float32 [8], P('wide'), may hold values from 0.5 to 2
- arc_size: float32 [16], replicated, may hold values from 0.5 to 2
- radial_size: float32 [16], replicated, may hold values from 0.3 to 1.5
- fdm_vectors: float32 [10, 10], replicated, may hold values from -2 to 2
- fdm_values: float32 [10], replicated, may hold values from 0.5 to 60
Outputs:
- velocity_out: float32 [3, 512, 4096], P(None, None, ('wide', 'narrow'))
- coarse_residual: float32 [3, 4352], P(None, ('wide', 'narrow'))
Inputs may be any that keep to these rules, and one draw needn't show every extreme that they name: `element_slot`: each device's row is a permutation of the block positions of its 128 elements. `corner_vertex`: the ids of a permutation of the 4352 vertices of the coarse grid (vertex at axial index, around index and radial offset 0 to 16, periodic along and around the pipe); corner a * 4 + b * 2 + c lies at axial offset a, around offset b, radial offset c of its element; elements that share a corner share its id.
All inputs are finite; a program needn't handle non-finite values.
Results may differ from a plain program's by a relative error of at most 0.0001.
Values sent between devices are 32-bit elements; how exact they have to be, the bound alone decides.
A program may use at most 128 MiB of HBM per device.

v0:
```python
from functools import partial

import jax
import jax.numpy as jnp
import ml_dtypes
import numpy as np
from jax import lax
from jax.experimental import pallas as pl
from jax.experimental.pallas import tpu as pltpu
from jax.sharding import PartitionSpec as P

AROUND_DEV = 8
RADIAL = 16
STEPS = 2
SIGMA = 4.0
VISCOSITY = 0.05
LIMIT = 48 * 1024 * 1024
MESH = pl.DeviceIdType.MESH
F32 = jnp.float32
BF16 = jnp.bfloat16


def node_tables():
    gll_nodes = np.array(
        [
            -1.0,
            -0.8717401485096066,
            -0.5917001814331423,
            -0.2092992179024789,
            0.2092992179024789,
            0.5917001814331423,
            0.8717401485096066,
            1.0,
        ]
    )
    gll_weights = np.array(
        [
            1.0 / 28.0,
            0.2107042271435061,
            0.3411226924835044,
            0.4124587946587038,
            0.4124587946587038,
            0.3411226924835044,
            0.2107042271435061,
            1.0 / 28.0,
        ]
    )
    bary_scale = np.array(
        [
            np.prod(
                [
                    gll_nodes[target] - gll_nodes[partner]
                    for partner in range(8)
                    if partner != target
                ]
            )
            for target in range(8)
        ]
    )
    derivative = np.zeros((8, 8))
    for target in range(8):
        for source in range(8):
            if target != source:
                derivative[target, source] = bary_scale[target] / (
                    bary_scale[source] * (gll_nodes[target] - gll_nodes[source])
                )
        derivative[target, target] = -np.sum(derivative[target])
    fine_nodes = np.array(
        [
            -0.9815606342467192,
            -0.9041172563704749,
            -0.7699026741943047,
            -0.5873179542866175,
            -0.3678314989981802,
            -0.1252334085114689,
            0.1252334085114689,
            0.3678314989981802,
            0.5873179542866175,
            0.7699026741943047,
            0.9041172563704749,
            0.9815606342467192,
        ]
    )
    fine_weights = np.array(
        [
            0.0471753363865118,
            0.1069393259953184,
            0.1600783285433462,
            0.2031674267230659,
            0.2334925365383548,
            0.2491470458134028,
            0.2491470458134028,
            0.2334925365383548,
            0.2031674267230659,
            0.1600783285433462,
            0.1069393259953184,
            0.0471753363865118,
        ]
    )
    interp = np.ones((12, 8))
    for source in range(8):
        for partner in range(8):
            if partner != source:
                interp[:, source] = (
                    interp[:, source]
                    * (fine_nodes - gll_nodes[partner])
                    / (gll_nodes[source] - gll_nodes[partner])
                )
    linear = np.stack([(1.0 - gll_nodes) / 2.0, (1.0 + gll_nodes) / 2.0])
    return derivative, interp, linear, gll_weights, fine_weights


def stack_const(matrix):
    high = matrix.astype(ml_dtypes.bfloat16)
    low = (matrix - high.astype(np.float64)).astype(ml_dtypes.bfloat16)
    return np.concatenate([high, low, high], axis=1)


DERIV, INTERP, LINEAR, WGLL, WFINE = node_tables()
INTERP_DERIV = INTERP @ DERIV
BEND = DERIV.T @ np.diag(WGLL) @ DERIV
FORWARD = stack_const(
    np.concatenate(
        [np.kron(INTERP, INTERP), np.kron(INTERP_DERIV, INTERP), np.kron(INTERP, INTERP_DERIV)]
    )
)
BACKWARD = stack_const((np.kron(INTERP, INTERP) * np.kron(WFINE, WFINE)[:, None]).T)
LINEAR_JK = stack_const(np.concatenate([np.kron(LINEAR[b], LINEAR[c])[None] for b in range(2) for c in range(2)] + [np.zeros((4, 64))]))
STIFF = stack_const(
    np.concatenate([np.kron(BEND, np.diag(WGLL)), np.kron(np.diag(WGLL), BEND)])
)
WEIGHT_JK = np.kron(WGLL, WGLL).astype(np.float32)


def split_rows(x):
    high = x.astype(BF16)
    low = (x - high.astype(F32)).astype(BF16)
    return jnp.concatenate([high, high, low], axis=0)


def split_cols(x):
    high = x.astype(BF16)
    low = (x - high.astype(F32)).astype(BF16)
    return jnp.concatenate([high, low, high], axis=1)


def mm(a, b):
    return jnp.dot(a, b, preferred_element_type=F32)


def combine(coefs, planes):
    total = None
    for coef, plane in zip(coefs, planes):
        term = plane * coef
        total = term if total is None else total + term
    return total


def lane_roll(x, shift):
    parts = [
        pltpu.roll(x[:, b : b + 128], shift, 1) for b in range(0, x.shape[1], 128)
    ]
    return jnp.concatenate(parts, axis=1)


def row_k(shape):
    return lax.broadcasted_iota(jnp.int32, shape, 0) % 8


def keep_mask(shape, low_in, high_in):
    k = row_k(shape)
    return jnp.where(k == 0, low_in, 1.0) * jnp.where(k == 7, high_in, 1.0)


def inverse_mult(shape, low_in, high_in, plane):
    k = row_k(shape)
    j = lax.broadcasted_iota(jnp.int32, shape, 0) // 8
    scale = jnp.where((j == 0) | (j == 7), 0.5, 1.0)
    scale = scale * jnp.where(k == 0, 1.0 - 0.5 * low_in, 1.0)
    scale = scale * jnp.where(k == 7, 1.0 - 0.5 * high_in, 1.0)
    return scale * 0.5 if plane in (0, 7) else scale


def around(mine, other, up):
    lane = lax.broadcasted_iota(jnp.int32, mine.shape, 1) % 128
    if up:
        return lane_roll(jnp.where(lane >= 128 - RADIAL, other, mine), RADIAL)
    return lane_roll(jnp.where(lane < RADIAL, other, mine), 128 - RADIAL)


def radial_sum(x, low_in, high_in):
    rows = x.shape[0]
    k = row_k(x.shape)
    below = lane_roll(pltpu.roll(x, rows - 7, 0), 1)
    above = lane_roll(pltpu.roll(x, 7, 0), 127)
    return x + jnp.where(k == 0, below * low_in, 0.0) + jnp.where(k == 7, above * high_in, 0.0)


def pack_faces(y, blocks, start):
    lane = lax.broadcasted_iota(jnp.int32, (8, 128), 1) // RADIAL
    packed = jnp.zeros((8, 128), F32)
    for q, (row, c) in enumerate(blocks):
        piece = y[row : row + 8, 128 * c : 128 * c + 128]
        packed = jnp.where(lane == q, pltpu.roll(piece, (RADIAL * q - start) % 128, 1), packed)
    return packed


def unpack_faces(packed, first, channels, start):
    return jnp.concatenate(
        [
            pltpu.roll(packed, (start - RADIAL * (first + c)) % 128, 1) if start != RADIAL * (first + c) else packed
            for c in range(channels)
        ],
        axis=1,
    )


def join_kernel(wide, x_ref, below_ref, above_ref, y_ref, prev_ref, next_ref):
    channels = x_ref.shape[2] // 128
    planes = [x_ref[i] for i in range(8)]
    if wide:
        planes = [below_ref[0], planes[0] + below_ref[1]] + planes[1:7]
        planes = planes + [x_ref[7] + above_ref[0], above_ref[1]]
        low_rows, high_rows = (0, 8), (48, 56)
    else:
        planes = [planes[0] + below_ref[0]] + planes[1:7] + [planes[7] + above_ref[0]]
        low_rows, high_rows = (0,), (56,)
    low = [(row, c) for row in low_rows for c in range(channels)]
    high = [(row, c) for row in high_rows for c in range(channels)]
    for i, plane in enumerate(planes):
        y_ref[i] = plane
        prev_ref[i] = pack_faces(plane, low, 0)
        next_ref[i] = pack_faces(plane, high, 128 - RADIAL)


def exact_parts(x):
    high = x.astype(BF16)
    rest = x - high.astype(F32)
    middle = rest.astype(BF16)
    return high, middle, (rest - middle.astype(F32)).astype(BF16)


def enter_kernel(vel_ref, slot_ref, mass_ref, field_ref):
    rows = lax.broadcasted_iota(jnp.int32, (128, 128), 0)
    place = jnp.where(rows == slot_ref[...], 1.0, 0.0).astype(BF16)
    for c in range(3):
        parts = exact_parts(vel_ref[c])
        moved = [
            lax.dot_general(p, place, (((1,), (1,)), ((), ())), preferred_element_type=F32)
            for p in parts
        ]
        lanes = slice(128 * c, 128 * c + 128)
        field_ref[:, lanes] = ((moved[0] + moved[1]) + moved[2]) * mass_ref[...]
    field_ref[:, 384:512] = mass_ref[...]


def leave_kernel(owners, u_ref, res_ref, slot_ref, ids_ref, ljk_ref, out_ref, full_ref):
    rows = lax.broadcasted_iota(jnp.int32, (128, 128), 0)
    place = jnp.where(rows == slot_ref[...], 1.0, 0.0).astype(BF16)
    for c in range(3):
        lanes = slice(128 * c, 128 * c + 128)
        moved = [mm(p, place) for p in exact_parts(u_ref[:, lanes])]
        out_ref[c] = (moved[0] + moved[1]) + moved[2]
    planes = [res_ref[64 * i : 64 * i + 64] for i in range(8)]
    corners = []
    for a in range(2):
        flat = combine([float(v) for v in LINEAR[a]], planes)
        corners.append(mm(ljk_ref[...], split_rows(flat))[0:4])
    corners = jnp.concatenate(corners, axis=0)
    share = AROUND_DEV * (RADIAL + 1)
    ids = ids_ref[...]
    owner = ids // share
    spot = ids - owner * share
    owner_rows = lax.broadcasted_iota(jnp.int32, (owners, 128), 0)
    spot_rows = lax.broadcasted_iota(jnp.int32, (256, 128), 0)
    left, right = [], []
    for q in range(8):
        hit = owner_rows == owner[q : q + 1]
        terms = []
        for c in range(3):
            value = corners[q : q + 1, 128 * c : 128 * c + 128]
            terms.append(jnp.where(hit, value, 0.0))
        left.append(jnp.concatenate(terms, axis=0))
        right.append(jnp.where(spot_rows == spot[q : q + 1], 1.0, 0.0).astype(BF16))
    left = jnp.concatenate(left, axis=1)
    right = jnp.concatenate(right, axis=1)
    parts = [
        lax.dot_general(p, right, (((1,), (1,)), ((), ())), preferred_element_type=F32)
        for p in exact_parts(left)
    ]
    full_ref[...] = (parts[0] + parts[1]) + parts[2]


def around_sum(y, prev_high, next_low):
    low = y[0:8] + around(y[56:64], prev_high, True)
    high = y[56:64] + around(y[0:8], next_low, False)
    return low, high


def stiffness(planes, index, geo, stiff, weight_jk):
    mixed = mm(stiff, split_rows(planes[index]))
    along = combine([float(v) for v in BEND[index]], planes) * weight_jk
    inv0, inv1, inv2 = geo[0:1], geo[1:2], geo[2:3]
    across = mixed[0:64] * (inv1 * inv1) + mixed[64:128] * (inv2 * inv2)
    return along * (inv0 * inv0) + across * float(WGLL[index])


def write_residual(u, geo, fwd_ref, back_ref, stiff_ref, wjk, out_ref, fine_ref):
    inv = [geo[d : d + 1, 0:128] for d in range(3)]
    volume, low_in, high_in = geo[3:4], geo[4:5], geo[5:6]
    fwd = fwd_ref[...]
    back = back_ref[...]
    stiff = stiff_ref[...]
    planes = [u[i] for i in range(8)]
    for a in range(12):
        plain = combine([float(v) for v in INTERP[a]], planes)
        slope = combine([float(v) for v in INTERP_DERIV[a]], planes)
        fine = mm(fwd, split_rows(plain))
        along = mm(fwd[0:144], split_rows(slope))
        speed = [fine[0:144, 128 * d : 128 * d + 128] * inv[d] for d in range(3)]
        terms = []
        for c in range(3):
            lanes = slice(128 * c, 128 * c + 128)
            terms.append(
                speed[0] * along[:, lanes]
                + speed[1] * fine[144:288, lanes]
                + speed[2] * fine[288:432, lanes]
            )
        fine_ref[a] = mm(back, split_rows(jnp.concatenate(terms, axis=1)))
    keep = keep_mask((64, 384), low_in, high_in)
    for i in range(8):
        advect = combine(
            [float(v) for v in INTERP[:, i] * WFINE], [fine_ref[a] for a in range(12)]
        )
        bend = stiffness(planes, i, geo, stiff, wjk)
        out_ref[i] = -(advect + VISCOSITY * bend) * volume * keep


def first_kernel(y_ref, prev_ref, next_ref, geo_ref, fwd, back, stiff, wjk_ref, u_ref, res_ref, fine_ref):
    geo = geo_ref[...]
    low4 = jnp.concatenate([geo[4:5], geo[4:5, 0:128]], axis=1)
    high4 = jnp.concatenate([geo[5:6], geo[5:6, 0:128]], axis=1)
    keep = keep_mask((64, 384), geo[4:5], geo[5:6])
    for i in range(8):
        y = y_ref[i]
        low, high = around_sum(y, unpack_faces(prev_ref[i], 0, 4, 112), unpack_faces(next_ref[i], 0, 4, 0))
        total = radial_sum(jnp.concatenate([low, y[8:56], high], axis=0), low4, high4)
        mass = total[:, 384:512]
        u_ref[i] = total[:, 0:384] / jnp.concatenate([mass, mass, mass], axis=1) * keep
    write_residual(u_ref, geo, fwd, back, stiff, wjk_ref[...], res_ref, fine_ref)


def next_kernel(u_in, dirn_ref, sums_ref, geo_ref, fwd, back, stiff, wjk_ref, u_ref, res_ref, fine_ref):
    sums = sums_ref[...]
    step = jnp.sum(sums[0:1], axis=1, keepdims=True) / jnp.sum(sums[1:2], axis=1, keepdims=True)
    for i in range(8):
        u_ref[i] = u_in[i] + dirn_ref[i] * step
    write_residual(u_ref, geo_ref[...], fwd, back, stiff, wjk_ref[...], res_ref, fine_ref)


def solve_kernel(y_ref, prev_ref, next_ref, geo_ref, s_ref, lam_ref, into_ref, back_ref, lam2_ref, res_ref, corr_ref, ext_ref, spec_ref):
    geo = geo_ref[...]
    volume, low_in, high_in = geo[3:4], geo[4:5], geo[5:6]
    into = split_cols(into_ref[...])
    back = split_cols(back_ref[...])
    for i in range(10):
        y = y_ref[i]
        prev, following = prev_ref[i], next_ref[i]
        low, high = around_sum(y, unpack_faces(prev, 3, 3, 112), unpack_faces(following, 0, 3, 0))
        outer_low = around(y[48:56], unpack_faces(prev, 0, 3, 112), True)
        outer_high = around(y[8:16], unpack_faces(following, 3, 3, 0), False)
        wide = jnp.concatenate([outer_low, low, y[8:56], high, outer_high], axis=0)
        wide = radial_sum(wide, low_in, high_in)
        if 1 <= i <= 8:
            res_ref[i - 1] = wide[8:72]
        k = row_k(wide.shape)
        halo = jnp.where(k == 6, lane_roll(wide, 1) * low_in, 0.0)
        halo = jnp.where(k == 1, lane_roll(wide, 127) * high_in, halo)
        ext_ref[i] = mm(into, split_rows(jnp.concatenate([wide, halo], axis=0)))
    sq = [geo[d : d + 1] * geo[d : d + 1] for d in range(3)]
    lam2 = lam2_ref[...]
    cross = (lam2[:, 0:1] * sq[1] + lam2[:, 1:2] * sq[2]) * VISCOSITY + SIGMA
    for a in range(10):
        spectral = combine([s_ref[i, a] for i in range(10)], [ext_ref[i] for i in range(10)])
        scaling = volume * (cross + (VISCOSITY * lam_ref[a]) * sq[0])
        spec_ref[a] = mm(back, split_rows(spectral / scaling))
    for i in range(8):
        corr = combine([s_ref[i + 1, a] for a in range(10)], [spec_ref[a] for a in range(10)])
        corr_ref[i] = corr * inverse_mult((64, 384), low_in, high_in, i)


def direction_kernel(y_ref, prev_ref, next_ref, res_ref, geo_ref, stiff_ref, wjk_ref, dirn_ref, sums_ref):
    geo = geo_ref[...]
    volume, low_in, high_in = geo[3:4], geo[4:5], geo[5:6]
    wjk = wjk_ref[...]
    stiff = stiff_ref[...]
    keep = keep_mask((64, 384), low_in, high_in)
    numer = jnp.zeros((64, 384), F32)
    for i in range(8):
        y = y_ref[i]
        low, high = around_sum(y, unpack_faces(prev_ref[i], 0, 3, 112), unpack_faces(next_ref[i], 0, 3, 0))
        total = radial_sum(jnp.concatenate([low, y[8:56], high], axis=0), low_in, high_in)
        total = total * keep
        dirn_ref[i] = total
        numer = numer + res_ref[i] * total * inverse_mult((64, 384), low_in, high_in, i)
    planes = [dirn_ref[i] for i in range(8)]
    denom = jnp.zeros((64, 384), F32)
    for i in range(8):
        bend = stiffness(planes, i, geo, stiff, wjk)
        mass = wjk * float(SIGMA * WGLL[i])
        denom = denom + planes[i] * (mass * planes[i] + VISCOSITY * bend)
    denom = denom * volume

    def fold(x):
        x = jnp.sum(x, axis=0, keepdims=True)
        return x[:, 0:128] + x[:, 128:256] + x[:, 256:384]

    row = lax.broadcasted_iota(jnp.int32, (8, 128), 0)
    sums_ref[...] = jnp.where(row == 0, fold(numer), jnp.where(row == 1, fold(denom), 0.0))


def sum_kernel(wide, narrow, scatter, x_ref, o_ref, from_narrow, part, from_wide, s1, r1, s2, r2):
    w, n = lax.axis_index("wide"), lax.axis_index("narrow")
    barrier = pltpu.get_barrier_semaphore()
    for k in range(1, narrow):
        pl.semaphore_signal(barrier, inc=1, device_id=(w, (n + k) % narrow), device_id_type=MESH)
    for k in range(1, wide):
        pl.semaphore_signal(barrier, inc=1, device_id=((w + k) % wide, n), device_id_type=MESH)
    pl.semaphore_wait(barrier, narrow + wide - 2)
    copies = []
    for k in range(1, narrow):
        peer = (n + k) % narrow
        copy = pltpu.make_async_remote_copy(
            src_ref=x_ref.at[peer] if scatter else x_ref,
            dst_ref=from_narrow.at[k - 1],
            send_sem=s1.at[k - 1],
            recv_sem=r1.at[k - 1],
            device_id=(w, peer),
            device_id_type=MESH,
        )
        copy.start()
        copies.append(copy)
    total = x_ref[n] if scatter else x_ref[...]
    for k, copy in enumerate(copies):
        copy.wait()
        total = total + from_narrow[k]
    part[...] = total
    copies = []
    for k in range(1, wide):
        peer = (w + k) % wide
        copy = pltpu.make_async_remote_copy(
            src_ref=part.at[peer] if scatter else part,
            dst_ref=from_wide.at[k - 1],
            send_sem=s2.at[k - 1],
            recv_sem=r2.at[k - 1],
            device_id=(peer, n),
            device_id_type=MESH,
        )
        copy.start()
        copies.append(copy)
    total = part[w] if scatter else part[...]
    for k, copy in enumerate(copies):
        copy.wait()
        total = total + from_wide[k]
    o_ref[...] = total


def device_sum(x, scatter, ident):
    wide, narrow = lax.axis_size("wide"), lax.axis_size("narrow")
    middle = x.shape[1:] if scatter else x.shape
    last = middle[1:] if scatter else x.shape
    return pl.pallas_call(
        partial(sum_kernel, wide, narrow, scatter),
        out_shape=jax.ShapeDtypeStruct(last, F32),
        in_specs=[pl.BlockSpec(memory_space=pltpu.VMEM)],
        out_specs=pl.BlockSpec(memory_space=pltpu.VMEM),
        scratch_shapes=[
            pltpu.VMEM((narrow - 1,) + middle, F32),
            pltpu.VMEM(middle, F32),
            pltpu.VMEM((wide - 1,) + last, F32),
            pltpu.SemaphoreType.DMA((narrow - 1,)),
            pltpu.SemaphoreType.DMA((narrow - 1,)),
            pltpu.SemaphoreType.DMA((wide - 1,)),
            pltpu.SemaphoreType.DMA((wide - 1,)),
        ],
        compiler_params=pltpu.CompilerParams(
            collective_id=ident, has_side_effects=True, vmem_limit_bytes=LIMIT
        ),
    )(x)


def local_call(body, args, outs, scratch, smem=()):
    return pl.pallas_call(
        body,
        out_shape=[jax.ShapeDtypeStruct(s, F32) for s in outs],
        in_specs=[
            pl.BlockSpec(memory_space=pltpu.SMEM if p in smem else pltpu.VMEM)
            for p in range(len(args))
        ],
        out_specs=[pl.BlockSpec(memory_space=pltpu.VMEM)] * len(outs),
        scratch_shapes=[pltpu.VMEM(s, F32) for s in scratch],
        compiler_params=pltpu.CompilerParams(vmem_limit_bytes=LIMIT),
    )(*args)


def swap(axis, to_prev, to_next):
    count = lax.axis_size(axis)
    from_prev = lax.ppermute(to_next, axis, [(i, (i + 1) % count) for i in range(count)])
    from_next = lax.ppermute(to_prev, axis, [((i + 1) % count, i) for i in range(count)])
    return from_prev, from_next


def exchange(x, wide=False):
    width = 2 if wide else 1
    below, above = swap("wide", x[0:width], x[8 - width : 8])
    depth = 10 if wide else 8
    y, low, high = local_call(
        partial(join_kernel, wide),
        (x, below, above),
        [(depth, 64, x.shape[2]), (depth, 8, 128), (depth, 8, 128)],
        [],
    )
    return (y,) + swap("narrow", low, high)


def shards(
    velocity,
    element_slot,
    corner_vertex,
    axial_size,
    arc_size,
    radial_size,
    fdm_vectors,
    fdm_values,
):
    wide_count, narrow_count = lax.axis_size("wide"), lax.axis_size("narrow")
    slot_of = element_slot[0]
    inverse_slot = jnp.zeros((128,), jnp.int32).at[slot_of].set(jnp.arange(128, dtype=jnp.int32))
    ids = corner_vertex[:, inverse_slot]
    er = jnp.arange(128) % RADIAL
    hz = jnp.broadcast_to(axial_size, (128,))
    ht = jnp.tile(arc_size, AROUND_DEV)
    hr = jnp.tile(radial_size, AROUND_DEV)
    volume = hz * ht * hr / 8.0
    zero = jnp.zeros((128,), F32)
    rows = [2.0 / hz, 2.0 / ht, 2.0 / hr, volume]
    rows += [jnp.where(er > 0, 1.0, 0.0), jnp.where(er < RADIAL - 1, 1.0, 0.0), zero, zero]
    geo = jnp.tile(jnp.stack(rows).astype(F32), (1, 3))
    fwd, back, stiff = jnp.asarray(FORWARD), jnp.asarray(BACKWARD), jnp.asarray(STIFF)
    wjk = jnp.broadcast_to(jnp.asarray(WEIGHT_JK)[:, None], (64, 384))
    consts = (geo, fwd, back, stiff, wjk)

    transform = fdm_vectors.T.reshape(10, 1, 10, 1) * fdm_vectors.T.reshape(1, 10, 1, 10)
    own = transform[..., 1:9].reshape(100, 80)
    halo = jnp.zeros((10, 10, 10, 8), F32)
    halo = halo.at[..., 6].set(transform[..., 0]).at[..., 1].set(transform[..., 9])
    into = jnp.pad(jnp.concatenate([own, halo.reshape(100, 80)], axis=1), ((0, 12), (0, 0)))
    inner = fdm_vectors[1:9]
    outof = (inner.reshape(8, 1, 10, 1) * inner.reshape(1, 8, 1, 10)).reshape(64, 100)
    outof = jnp.pad(outof, ((0, 0), (0, 12)))
    lam2 = jnp.stack([jnp.repeat(fdm_values, 10), jnp.tile(fdm_values, 10)], axis=1)
    lam2 = jnp.pad(lam2, ((0, 12), (0, 126)), constant_values=1.0)

    mass = (np.kron(WGLL, np.kron(WGLL, WGLL)).astype(np.float32))[:, None] * volume[None]
    (field,) = local_call(enter_kernel, (velocity, element_slot, mass), [(512, 512)], [])
    field = field.reshape(8, 64, 512)

    shape = (8, 64, 384)
    u, res = local_call(first_kernel, exchange(field) + consts, [shape, shape], [(12, 64, 384)])
    for step in range(STEPS):
        total, corr = local_call(
            solve_kernel,
            exchange(res, True) + (geo, fdm_vectors, fdm_values, into, outof, lam2),
            [shape, shape],
            [(10, 112, 384), (10, 64, 384)],
            smem=(4, 5),
        )
        dirn, sums = local_call(
            direction_kernel, exchange(corr) + (total, geo, stiff, wjk), [shape, (8, 128)], []
        )
        sums = device_sum(sums, False, step)
        u, res = local_call(
            next_kernel, (u, dirn, sums) + consts, [shape, shape], [(12, 64, 384)]
        )
    owners = wide_count * narrow_count
    share = AROUND_DEV * (RADIAL + 1)
    out, full = local_call(
        partial(leave_kernel, owners),
        (u.reshape(512, 384), res.reshape(512, 384), element_slot, ids, jnp.asarray(LINEAR_JK)),
        [(3, 512, 128), (3 * owners, 256)],
        [],
    )
    blocks = full.reshape(3, wide_count, narrow_count, 256).transpose(2, 1, 0, 3)
    blocks = jnp.pad(blocks, ((0, 0), (0, 0), (0, 5), (0, 0)))
    coarse = device_sum(blocks, True, STEPS)[0:3, 0:share]
    return out, coarse


def solution(mesh):
    return jax.shard_map(
        shards,
        mesh=mesh,
        in_specs=(
            P(None, None, ("wide", "narrow")),
            P(("wide", "narrow"), None),
            P(None, ("wide", "narrow")),
            P("wide"),
            P(),
            P(),
            P(),
            P(),
        ),
        out_specs=(P(None, None, ("wide", "narrow")), P(None, ("wide", "narrow"))),
        check_vma=False,
    )
```

profile of v0, /device:TPU:0, one launch (start us, length us, event | category | flops | bytes accessed | tf_op | source)
XLA Modules:
  0.0 141.6 jit_solution(5164262427767702318)
XLA Ops:
  1.3 0.6 copy-done.14
  2.1 0.6 copy-done.12
  2.6 0.1 broadcast_multiply_fusion.2.mass_ref
  2.8 0.5 copy-done.9
  3.3 1.1 copy-done.2
  4.4 0.5 shard_map.149
  5.0 3.0 %collective-permute-start = (f32[1,64,512]{2,1,0:T(8,128)S(1)}, f32[1,64,512]{2,1,0:T(8,128)S(1)}, u32[]{:S(2)}, u32[]{:S(2)}) collective-permute-start(f32[1,64,512]{2,1,0:T(8,128)S(1)} %get-tuple-element.89), channel_id=1, source_target_pairs={{0,4},{4,8},{8,12},{12,16},{16,20},{20,24},{24,28},{28,0},{1,5},{5... | collective-permute-start | bytes 393224 | tf_op jit(solution)/shard_map/ppermute | solution.py:508
  8.0 3.1 %collective-permute-start.1 = (f32[1,64,512]{2,1,0:T(8,128)S(1)}, f32[1,64,512]{2,1,0:T(8,128)S(1)}, u32[]{:S(2)}, u32[]{:S(2)}) collective-permute-start(f32[1,64,512]{2,1,0:T(8,128)S(1)} %get-tuple-element.88), channel_id=1, source_target_pairs={{4,0},{8,4},{12,8},{16,12},{20,16},{24,20},{28,24},{0,28},{5,1},{9... | collective-permute-start | bytes 393224 | tf_op jit(solution)/shard_map/ppermute | solution.py:509
  11.2 0.1 broadcast_multiply_fusion
  11.5 0.9 scatter.14
  12.4 0.6 slice_dynamic-update-slice_fusion
  13.1 1.3 reshape.237
  14.5 0.2 reshape.236
  15.0 0.8 collective-permute-done.1.above_ref
  15.8 0.1 shard_map.150
  16.0 1.7 %collective-permute-start.3 = (f32[8,8,128]{2,1,0:T(8,128)S(1)}, f32[8,8,128]{2,1,0:T(8,128)S(1)}, u32[]{:S(2)}, u32[]{:S(2)}) collective-permute-start(f32[8,8,128]{2,1,0:T(8,128)S(1)} %get-tuple-element.59), channel_id=1, source_target_pairs={{1,0},{2,1},{3,2},{0,3},{5,4},{6,5},{7,6},{4,7},{9,8},{10,9},{11,1... | collective-permute-start | bytes 98312 | tf_op jit(solution)/shard_map/ppermute | solution.py:509
  17.9 0.6 copy-done.7
  18.7 0.6 collective-permute-done.2.prev_ref
  19.4 6.9 %shard_map.151 = (f32[8,64,384]{2,1,0:T(8,128)S(1)}, f32[8,64,384]{2,1,0:T(8,128)S(1)}) custom-call(f32[8,64,512]{2,1,0:T(8,128)S(1)} %get-tuple-element.57.y_ref, f32[8,8,128]{2,1,0:T(8,128)S(1)} %collective-permute-done.2.prev_ref, f32[8,8,128]{2,1,0:T(8,128)S(1)} %collective-permute-done.3.next_ref, f32[8,384]{1,0:T(8,128)S(1)} %broadcast_bitcast_fusion.geo_ref, ...), custom_call_target="tpu_custom_call" | custom-call | tf_op jit(solution)/shard_map/pallas_call | solution.py:493
  26.4 0.3 collective-permute-start.4
  26.7 4.5 %collective-permute-start.5 = (f32[2,64,384]{2,1,0:T(8,128)S(1)}, f32[2,64,384]{2,1,0:T(8,128)S(1)}, u32[]{:S(2)}, u32[]{:S(2)}) collective-permute-start(f32[2,64,384]{2,1,0:T(8,128)S(1)} %get-tuple-element.96), channel_id=1, source_target_pairs={{4,0},{8,4},{12,8},{16,12},{20,16},{24,20},{28,24},{0,28},{5,1},{9... | collective-permute-start | bytes 589832 | tf_op jit(solution)/shard_map/ppermute | solution.py:509
  31.3 5.2 %collective-permute-done.4.below_ref = f32[2,64,384]{2,1,0:T(8,128)S(1)} collective-permute-done((f32[2,64,384]{2,1,0:T(8,128)S(1)}, f32[2,64,384]{2,1,0:T(8,128)S(1)}, u32[]{:S(2)}, u32[]{:S(2)}) %collective-permute-start.4) | collective-permute-done | bytes 196640 | tf_op jit(solution)/shard_map/ppermute | solution.py:508
  36.5 2.1 %collective-permute-done.5.above_ref = f32[2,64,384]{2,1,0:T(8,128)S(1)} collective-permute-done((f32[2,64,384]{2,1,0:T(8,128)S(1)}, f32[2,64,384]{2,1,0:T(8,128)S(1)}, u32[]{:S(2)}, u32[]{:S(2)}) %collective-permute-start.5) | collective-permute-done | bytes 196640 | tf_op jit(solution)/shard_map/ppermute | solution.py:509
  38.5 0.2 shard_map.152
  38.7 0.5 collective-permute-start.6
  39.2 1.3 collective-permute-start.7
  40.5 0.2 mul.87
  40.8 0.1 copy.37
  40.9 1.3 collective-permute-done.6.prev_ref
  42.2 5.0 %shard_map.153 = (f32[8,64,384]{2,1,0:T(8,128)S(1)}, f32[8,64,384]{2,1,0:T(8,128)S(1)}) custom-call(f32[10,64,384]{2,1,0:T(8,128)S(1)} %get-tuple-element.62.y_ref, f32[10,8,128]{2,1,0:T(8,128)S(1)} %collective-permute-done.6.prev_ref, f32[10,8,128]{2,1,0:T(8,128)S(1)} %collective-permute-done.7.next_ref, f32[8,384]{1,0:T(8,128)S(1)} %broadcast_bitcast_fusion.geo_ref, ...), custom_call_target="tpu_custom_call" | custom-call | tf_op jit(solution)/shard_map/pallas_call | solution.py:493
  47.3 4.7 %collective-permute-start.9 = (f32[1,64,384]{2,1,0:T(8,128)S(1)}, f32[1,64,384]{2,1,0:T(8,128)S(1)}, u32[]{:S(2)}, u32[]{:S(2)}) collective-permute-start(f32[1,64,384]{2,1,0:T(8,128)S(1)} %get-tuple-element.94), channel_id=1, source_target_pairs={{4,0},{8,4},{12,8},{16,12},{20,16},{24,20},{28,24},{0,28},{5,1},{9... | collective-permute-start | bytes 294920 | tf_op jit(solution)/shard_map/ppermute | solution.py:509
  52.0 2.8 %collective-permute-done.8.below_ref = f32[1,64,384]{2,1,0:T(8,128)S(1)} collective-permute-done((f32[1,64,384]{2,1,0:T(8,128)S(1)}, f32[1,64,384]{2,1,0:T(8,128)S(1)}, u32[]{:S(2)}, u32[]{:S(2)}) %collective-permute-start.8) | collective-permute-done | bytes 98336 | tf_op jit(solution)/shard_map/ppermute | solution.py:508
  54.9 1.4 collective-permute-done.9.above_ref
  56.2 0.1 shard_map.154
  56.4 0.2 collective-permute-start.10
  56.5 1.6 %collective-permute-start.11 = (f32[8,8,128]{2,1,0:T(8,128)S(1)}, f32[8,8,128]{2,1,0:T(8,128)S(1)}, u32[]{:S(2)}, u32[]{:S(2)}) collective-permute-start(f32[8,8,128]{2,1,0:T(8,128)S(1)} %get-tuple-element.68), channel_id=1, source_target_pairs={{1,0},{2,1},{3,2},{0,3},{5,4},{6,5},{7,6},{4,7},{9,8},{10,9},{11,1... | collective-permute-start | bytes 98312 | tf_op jit(solution)/shard_map/ppermute | solution.py:509
  58.2 1.6 %collective-permute-done.10.prev_ref = f32[8,8,128]{2,1,0:T(8,128)S(1)} collective-permute-done((f32[8,8,128]{2,1,0:T(8,128)S(1)}, f32[8,8,128]{2,1,0:T(8,128)S(1)}, u32[]{:S(2)}, u32[]{:S(2)}) %collective-permute-start.10) | collective-permute-done | bytes 32800 | tf_op jit(solution)/shard_map/ppermute | solution.py:508
  59.8 1.6 %shard_map.155 = (f32[8,64,384]{2,1,0:T(8,128)S(1)}, f32[8,128]{1,0:T(8,128)S(1)}) custom-call(f32[8,64,384]{2,1,0:T(8,128)S(1)} %get-tuple-element.66.y_ref, f32[8,8,128]{2,1,0:T(8,128)S(1)} %collective-permute-done.10.prev_ref, f32[8,8,128]{2,1,0:T(8,128)S(1)} %collective-permute-done.11.next_ref, f32[8,64,384]{2,1,0:T(8,128)S(1)} %get-tuple-element.69.res_ref, ...), custom_call_target="tpu_custom_call" | custom-call | tf_op jit(solution)/shard_map/pallas_call | solution.py:493
  61.4 10.2 %shard_map.156.sums_ref = f32[8,128]{1,0:T(8,128)S(1)} custom-call(f32[8,128]{1,0:T(8,128)S(1)} %get-tuple-element.71.x_ref), custom_call_target="tpu_custom_call" | custom-call | tf_op jit(solution)/shard_map/pallas_call | solution.py:472
  71.6 6.2 %shard_map.157 = (f32[8,64,384]{2,1,0:T(8,128)S(1)}, f32[8,64,384]{2,1,0:T(8,128)S(1)}) custom-call(f32[8,64,384]{2,1,0:T(8,128)S(1)} %get-tuple-element.60.u_in, f32[8,64,384]{2,1,0:T(8,128)S(1)} %get-tuple-element.70.dirn_ref, f32[8,128]{1,0:T(8,128)S(1)} %shard_map.156.sums_ref, f32[8,384]{1,0:T(8,128)S(1)} %broadcast_bitcast_fusion.geo_ref, ...), custom_call_target="tpu_custom_call" | custom-call | tf_op jit(solution)/shard_map/pallas_call | solution.py:493
  77.8 0.6 collective-permute-start.12
  78.5 4.1 %collective-permute-start.13 = (f32[2,64,384]{2,1,0:T(8,128)S(1)}, f32[2,64,384]{2,1,0:T(8,128)S(1)}, u32[]{:S(2)}, u32[]{:S(2)}) collective-permute-start(f32[2,64,384]{2,1,0:T(8,128)S(1)} %get-tuple-element.92), channel_id=1, source_target_pairs={{4,0},{8,4},{12,8},{16,12},{20,16},{24,20},{28,24},{0,28},{5,1},{9... | collective-permute-start | bytes 589832 | tf_op jit(solution)/shard_map/ppermute | solution.py:509
  82.6 4.1 %collective-permute-done.12.below_ref = f32[2,64,384]{2,1,0:T(8,128)S(1)} collective-permute-done((f32[2,64,384]{2,1,0:T(8,128)S(1)}, f32[2,64,384]{2,1,0:T(8,128)S(1)}, u32[]{:S(2)}, u32[]{:S(2)}) %collective-permute-start.12) | collective-permute-done | bytes 196640 | tf_op jit(solution)/shard_map/ppermute | solution.py:508
  86.8 2.0 %collective-permute-done.13.above_ref = f32[2,64,384]{2,1,0:T(8,128)S(1)} collective-permute-done((f32[2,64,384]{2,1,0:T(8,128)S(1)}, f32[2,64,384]{2,1,0:T(8,128)S(1)}, u32[]{:S(2)}, u32[]{:S(2)}) %collective-permute-start.13) | collective-permute-done | bytes 196640 | tf_op jit(solution)/shard_map/ppermute | solution.py:509
  88.8 0.2 shard_map.158
  89.0 1.7 %collective-permute-start.15 = (f32[10,8,128]{2,1,0:T(8,128)S(1)}, f32[10,8,128]{2,1,0:T(8,128)S(1)}, u32[]{:S(2)}, u32[]{:S(2)}) collective-permute-start(f32[10,8,128]{2,1,0:T(8,128)S(1)} %get-tuple-element.76), channel_id=1, source_target_pairs={{1,0},{2,1},{3,2},{0,3},{5,4},{6,5},{7,6},{4,7},{9,8},{10,9},{11,1... | collective-permute-start | bytes 122888 | tf_op jit(solution)/shard_map/ppermute | solution.py:509
  90.8 1.0 scatter_custom_fusion
  91.8 0.7 collective-permute-done.14.prev_ref
  92.5 5.0 %shard_map.159 = (f32[8,64,384]{2,1,0:T(8,128)S(1)}, f32[8,64,384]{2,1,0:T(8,128)S(1)}) custom-call(f32[10,64,384]{2,1,0:T(8,128)S(1)} %get-tuple-element.74.y_ref, f32[10,8,128]{2,1,0:T(8,128)S(1)} %collective-permute-done.14.prev_ref, f32[10,8,128]{2,1,0:T(8,128)S(1)} %collective-permute-done.15.next_ref, f32[8,384]{1,0:T(8,128)S(1)} %broadcast_bitcast_fusion.geo_ref, ...), custom_call_target="tpu_custom_call" | custom-call | tf_op jit(solution)/shard_map/pallas_call | solution.py:493
  97.5 0.3 collective-permute-start.16
  97.9 4.4 %collective-permute-start.17 = (f32[1,64,384]{2,1,0:T(8,128)S(1)}, f32[1,64,384]{2,1,0:T(8,128)S(1)}, u32[]{:S(2)}, u32[]{:S(2)}) collective-permute-start(f32[1,64,384]{2,1,0:T(8,128)S(1)} %get-tuple-element.90), channel_id=1, source_target_pairs={{4,0},{8,4},{12,8},{16,12},{20,16},{24,20},{28,24},{0,28},{5,1},{9... | collective-permute-start | bytes 294920 | tf_op jit(solution)/shard_map/ppermute | solution.py:509
  102.3 3.6 %collective-permute-done.16.below_ref = f32[1,64,384]{2,1,0:T(8,128)S(1)} collective-permute-done((f32[1,64,384]{2,1,0:T(8,128)S(1)}, f32[1,64,384]{2,1,0:T(8,128)S(1)}, u32[]{:S(2)}, u32[]{:S(2)}) %collective-permute-start.16) | collective-permute-done | bytes 98336 | tf_op jit(solution)/shard_map/ppermute | solution.py:508
  105.9 0.1 shard_map.160
  106.0 0.2 collective-permute-start.18
  106.2 1.6 %collective-permute-start.19 = (f32[8,8,128]{2,1,0:T(8,128)S(1)}, f32[8,8,128]{2,1,0:T(8,128)S(1)}, u32[]{:S(2)}, u32[]{:S(2)}) collective-permute-start(f32[8,8,128]{2,1,0:T(8,128)S(1)} %get-tuple-element.80), channel_id=1, source_target_pairs={{1,0},{2,1},{3,2},{0,3},{5,4},{6,5},{7,6},{4,7},{9,8},{10,9},{11,1... | collective-permute-start | bytes 98312 | tf_op jit(solution)/shard_map/ppermute | solution.py:509
  107.9 0.6 gather_fusion
  108.6 0.8 collective-permute-done.18.prev_ref
  109.4 1.6 %shard_map.161 = (f32[8,64,384]{2,1,0:T(8,128)S(1)}, f32[8,128]{1,0:T(8,128)S(1)}) custom-call(f32[8,64,384]{2,1,0:T(8,128)S(1)} %get-tuple-element.78.y_ref, f32[8,8,128]{2,1,0:T(8,128)S(1)} %collective-permute-done.18.prev_ref, f32[8,8,128]{2,1,0:T(8,128)S(1)} %collective-permute-done.19.next_ref, f32[8,64,384]{2,1,0:T(8,128)S(1)} %get-tuple-element.81.res_ref, ...), custom_call_target="tpu_custom_call" | custom-call | tf_op jit(solution)/shard_map/pallas_call | solution.py:493
  111.0 10.8 %shard_map.162.sums_ref = f32[8,128]{1,0:T(8,128)S(1)} custom-call(f32[8,128]{1,0:T(8,128)S(1)} %get-tuple-element.83.x_ref), custom_call_target="tpu_custom_call" | custom-call | tf_op jit(solution)/shard_map/pallas_call | solution.py:472
  121.9 6.2 %shard_map.163 = (f32[8,64,384]{2,1,0:T(8,128)S(1)}, f32[8,64,384]{2,1,0:T(8,128)S(1)}) custom-call(f32[8,64,384]{2,1,0:T(8,128)S(1)} %copy-done.4, f32[8,64,384]{2,1,0:T(8,128)S(1)} %get-tuple-element.82.dirn_ref, f32[8,128]{1,0:T(8,128)S(1)} %shard_map.162.sums_ref, f32[8,384]{1,0:T(8,128)S(1)} %broadcast_bitcast_fusion.geo_ref, ...), custom_call_target="tpu_custom_call" | custom-call | tf_op jit(solution)/shard_map/pallas_call | solution.py:493
  128.1 0.7 copy-done.8
  128.8 1.7 %shard_map.164 = (f32[3,512,128]{2,1,0:T(8,128)}, f32[96,256]{1,0:T(8,128)S(1)}) custom-call(f32[512,384]{1,0:T(8,128)S(1)} %bitcast.30, f32[512,384]{1,0:T(8,128)S(1)} %bitcast.31, s32[1,128]{1,0:T(1,128)S(1)} %copy-done.9, s32[8,128]{1,0:T(8,128)S(1)} %bitcast.33, bf16[8,192]{1,0:T(8,128)(2,1)S(1)} %copy-done.8), custom_call_target="tpu_custom_call" | custom-call | tf_op jit(solution)/shard_map/pallas_call | solution.py:493
  130.6 10.4 %shard_map.165 = f32[8,256]{1,0:T(8,128)S(1)} custom-call(f32[4,8,8,256]{3,2,1,0:T(8,128)S(1)} %pad.24.x_ref), custom_call_target="tpu_custom_call" | custom-call | tf_op jit(solution)/shard_map/pallas_call | solution.py:472
  141.0 0.6 slice.116
  (81 shorter events, 1.9 us)
Async XLA Ops:
  1.3 0.7 copy-start.14
  1.3 0.7 copy-start.15
  2.0 0.7 copy-start.12
  2.6 0.7 copy-start.9
  3.3 1.1 copy-start.2
  5.0 6.2 %copy-start.6 = (f32[10,10]{1,0:T(8,128)S(1)}, f32[10,10]{1,0:T(8,128)}, u32[]{:S(2)}) copy-start(f32[10,10]{1,0:T(8,128)} %s_ref.3) | copy-start | bytes 1204
  5.0 10.0 %collective-permute-start = (f32[1,64,512]{2,1,0:T(8,128)S(1)}, f32[1,64,512]{2,1,0:T(8,128)S(1)}, u32[]{:S(2)}, u32[]{:S(2)}) collective-permute-start(f32[1,64,512]{2,1,0:T(8,128)S(1)} %get-tuple-element.89), channel_id=1, source_target_pairs={{0,4},{4,8},{8,12},{12,16},{16,20},{20,24},{24,28},{28,0},{1,5},{5... | collective-permute-start | bytes 393224 | tf_op jit(solution)/shard_map/ppermute | solution.py:508
  8.0 7.8 %collective-permute-start.1 = (f32[1,64,512]{2,1,0:T(8,128)S(1)}, f32[1,64,512]{2,1,0:T(8,128)S(1)}, u32[]{:S(2)}, u32[]{:S(2)}) collective-permute-start(f32[1,64,512]{2,1,0:T(8,128)S(1)} %get-tuple-element.88), channel_id=1, source_target_pairs={{4,0},{8,4},{12,8},{16,12},{20,16},{24,20},{28,24},{0,28},{5,1},{9... | collective-permute-start | bytes 393224 | tf_op jit(solution)/shard_map/ppermute | solution.py:509
  11.3 1.1 copy-start.10
  13.1 1.4 %slice-start = ((f32[10,10,10,10]{1,0,3,2:T(8,128)}), f32[10,10,10,8]{1,0,3,2:T(8,128)S(1)}, s32[]{:S(2)}) async-start(f32[10,10,10,10]{1,0,3,2:T(8,128)} %copy-done.10), calls=%async_computation | async-start | bytes 1310720 | tf_op jit(solution)/shard_map/slice | solution.py:554
  15.9 3.5 %copy-start = (bf16[432,192]{1,0:T(8,128)(2,1)S(1)}, bf16[432,192]{1,0:T(8,128)(2,1)}, u32[]{:S(2)}) copy-start(bf16[432,192]{1,0:T(8,128)(2,1)} %constant.99.clone.fwd) | copy-start | bytes 497668
  15.9 3.4 %collective-permute-start.2 = (f32[8,8,128]{2,1,0:T(8,128)S(1)}, f32[8,8,128]{2,1,0:T(8,128)S(1)}, u32[]{:S(2)}, u32[]{:S(2)}) collective-permute-start(f32[8,8,128]{2,1,0:T(8,128)S(1)} %get-tuple-element.58), channel_id=1, source_target_pairs={{0,1},{1,2},{2,3},{3,0},{4,5},{5,6},{6,7},{7,4},{8,9},{9,10},{10,1... | collective-permute-start | bytes 98312 | tf_op jit(solution)/shard_map/ppermute | solution.py:508
  16.0 3.3 %collective-permute-start.3 = (f32[8,8,128]{2,1,0:T(8,128)S(1)}, f32[8,8,128]{2,1,0:T(8,128)S(1)}, u32[]{:S(2)}, u32[]{:S(2)}) collective-permute-start(f32[8,8,128]{2,1,0:T(8,128)S(1)} %get-tuple-element.59), channel_id=1, source_target_pairs={{1,0},{2,1},{3,2},{0,3},{5,4},{6,5},{7,6},{4,7},{9,8},{10,9},{11,1... | collective-permute-start | bytes 98312 | tf_op jit(solution)/shard_map/ppermute | solution.py:509
  17.7 1.6 %copy-start.13 = (f32[64]{0:T(128)S(1)}, f32[64]{0:T(128)}, u32[]{:S(2)}) copy-start(f32[64]{0:T(128)} %constant.102.clone) | copy-start | bytes 772
  17.8 0.7 copy-start.7
  18.5 0.9 copy-start.5
  18.5 0.9 copy-start.1
  26.4 10.0 %collective-permute-start.4 = (f32[2,64,384]{2,1,0:T(8,128)S(1)}, f32[2,64,384]{2,1,0:T(8,128)S(1)}, u32[]{:S(2)}, u32[]{:S(2)}) collective-permute-start(f32[2,64,384]{2,1,0:T(8,128)S(1)} %get-tuple-element.97), channel_id=1, source_target_pairs={{0,4},{4,8},{8,12},{12,16},{16,20},{20,24},{24,28},{28,0},{1,5},{5... | collective-permute-start | bytes 589832 | tf_op jit(solution)/shard_map/ppermute | solution.py:508
  26.7 11.8 %collective-permute-start.5 = (f32[2,64,384]{2,1,0:T(8,128)S(1)}, f32[2,64,384]{2,1,0:T(8,128)S(1)}, u32[]{:S(2)}, u32[]{:S(2)}) collective-permute-start(f32[2,64,384]{2,1,0:T(8,128)S(1)} %get-tuple-element.96), channel_id=1, source_target_pairs={{4,0},{8,4},{12,8},{16,12},{20,16},{24,20},{28,24},{0,28},{5,1},{9... | collective-permute-start | bytes 589832 | tf_op jit(solution)/shard_map/ppermute | solution.py:509
  38.7 3.5 %collective-permute-start.6 = (f32[10,8,128]{2,1,0:T(8,128)S(1)}, f32[10,8,128]{2,1,0:T(8,128)S(1)}, u32[]{:S(2)}, u32[]{:S(2)}) collective-permute-start(f32[10,8,128]{2,1,0:T(8,128)S(1)} %get-tuple-element.63), channel_id=1, source_target_pairs={{0,1},{1,2},{2,3},{3,0},{4,5},{5,6},{6,7},{7,4},{8,9},{9,10},{10,1... | collective-permute-start | bytes 122888 | tf_op jit(solution)/shard_map/ppermute | solution.py:508
  39.2 3.0 %collective-permute-start.7 = (f32[10,8,128]{2,1,0:T(8,128)S(1)}, f32[10,8,128]{2,1,0:T(8,128)S(1)}, u32[]{:S(2)}, u32[]{:S(2)}) collective-permute-start(f32[10,8,128]{2,1,0:T(8,128)S(1)} %get-tuple-element.64), channel_id=1, source_target_pairs={{1,0},{2,1},{3,2},{0,3},{5,4},{6,5},{7,6},{4,7},{9,8},{10,9},{11,1... | collective-permute-start | bytes 122888 | tf_op jit(solution)/shard_map/ppermute | solution.py:509
  47.3 7.6 %collective-permute-start.8 = (f32[1,64,384]{2,1,0:T(8,128)S(1)}, f32[1,64,384]{2,1,0:T(8,128)S(1)}, u32[]{:S(2)}, u32[]{:S(2)}) collective-permute-start(f32[1,64,384]{2,1,0:T(8,128)S(1)} %get-tuple-element.95), channel_id=1, source_target_pairs={{0,4},{4,8},{8,12},{12,16},{16,20},{20,24},{24,28},{28,0},{1,5},{5... | collective-permute-start | bytes 294920 | tf_op jit(solution)/shard_map/ppermute | solution.py:508
  47.3 8.9 %collective-permute-start.9 = (f32[1,64,384]{2,1,0:T(8,128)S(1)}, f32[1,64,384]{2,1,0:T(8,128)S(1)}, u32[]{:S(2)}, u32[]{:S(2)}) collective-permute-start(f32[1,64,384]{2,1,0:T(8,128)S(1)} %get-tuple-element.94), channel_id=1, source_target_pairs={{4,0},{8,4},{12,8},{16,12},{20,16},{24,20},{28,24},{0,28},{5,1},{9... | collective-permute-start | bytes 294920 | tf_op jit(solution)/shard_map/ppermute | solution.py:509
  56.4 3.4 %collective-permute-start.10 = (f32[8,8,128]{2,1,0:T(8,128)S(1)}, f32[8,8,128]{2,1,0:T(8,128)S(1)}, u32[]{:S(2)}, u32[]{:S(2)}) collective-permute-start(f32[8,8,128]{2,1,0:T(8,128)S(1)} %get-tuple-element.67), channel_id=1, source_target_pairs={{0,1},{1,2},{2,3},{3,0},{4,5},{5,6},{6,7},{7,4},{8,9},{9,10},{10,1... | collective-permute-start | bytes 98312 | tf_op jit(solution)/shard_map/ppermute | solution.py:508
  56.5 3.2 %collective-permute-start.11 = (f32[8,8,128]{2,1,0:T(8,128)S(1)}, f32[8,8,128]{2,1,0:T(8,128)S(1)}, u32[]{:S(2)}, u32[]{:S(2)}) collective-permute-start(f32[8,8,128]{2,1,0:T(8,128)S(1)} %get-tuple-element.68), channel_id=1, source_target_pairs={{1,0},{2,1},{3,2},{0,3},{5,4},{6,5},{7,6},{4,7},{9,8},{10,9},{11,1... | collective-permute-start | bytes 98312 | tf_op jit(solution)/shard_map/ppermute | solution.py:509
  77.8 9.0 %copy-start.3 = (f32[8,64,384]{2,1,0:T(8,128)}, f32[8,64,384]{2,1,0:T(8,128)S(1)}, u32[]{:S(2)}) copy-start(f32[8,64,384]{2,1,0:T(8,128)S(1)} %get-tuple-element.72.u_in) | copy-start | bytes 2359300
  77.8 8.9 %collective-permute-start.12 = (f32[2,64,384]{2,1,0:T(8,128)S(1)}, f32[2,64,384]{2,1,0:T(8,128)S(1)}, u32[]{:S(2)}, u32[]{:S(2)}) collective-permute-start(f32[2,64,384]{2,1,0:T(8,128)S(1)} %get-tuple-element.93), channel_id=1, source_target_pairs={{0,4},{4,8},{8,12},{12,16},{16,20},{20,24},{24,28},{28,0},{1,5},{5... | collective-permute-start | bytes 589832 | tf_op jit(solution)/shard_map/ppermute | solution.py:508
  78.5 10.3 %collective-permute-start.13 = (f32[2,64,384]{2,1,0:T(8,128)S(1)}, f32[2,64,384]{2,1,0:T(8,128)S(1)}, u32[]{:S(2)}, u32[]{:S(2)}) collective-permute-start(f32[2,64,384]{2,1,0:T(8,128)S(1)} %get-tuple-element.92), channel_id=1, source_target_pairs={{4,0},{8,4},{12,8},{16,12},{20,16},{24,20},{28,24},{0,28},{5,1},{9... | collective-permute-start | bytes 589832 | tf_op jit(solution)/shard_map/ppermute | solution.py:509
  89.0 3.5 %collective-permute-start.14 = (f32[10,8,128]{2,1,0:T(8,128)S(1)}, f32[10,8,128]{2,1,0:T(8,128)S(1)}, u32[]{:S(2)}, u32[]{:S(2)}) collective-permute-start(f32[10,8,128]{2,1,0:T(8,128)S(1)} %get-tuple-element.75), channel_id=1, source_target_pairs={{0,1},{1,2},{2,3},{3,0},{4,5},{5,6},{6,7},{7,4},{8,9},{9,10},{10,1... | collective-permute-start | bytes 122888 | tf_op jit(solution)/shard_map/ppermute | solution.py:508
  89.0 3.4 %collective-permute-start.15 = (f32[10,8,128]{2,1,0:T(8,128)S(1)}, f32[10,8,128]{2,1,0:T(8,128)S(1)}, u32[]{:S(2)}, u32[]{:S(2)}) collective-permute-start(f32[10,8,128]{2,1,0:T(8,128)S(1)} %get-tuple-element.76), channel_id=1, source_target_pairs={{1,0},{2,1},{3,2},{0,3},{5,4},{6,5},{7,6},{4,7},{9,8},{10,9},{11,1... | collective-permute-start | bytes 122888 | tf_op jit(solution)/shard_map/ppermute | solution.py:509
  97.5 8.3 %collective-permute-start.16 = (f32[1,64,384]{2,1,0:T(8,128)S(1)}, f32[1,64,384]{2,1,0:T(8,128)S(1)}, u32[]{:S(2)}, u32[]{:S(2)}) collective-permute-start(f32[1,64,384]{2,1,0:T(8,128)S(1)} %get-tuple-element.91), channel_id=1, source_target_pairs={{0,4},{4,8},{8,12},{12,16},{16,20},{20,24},{24,28},{28,0},{1,5},{5... | collective-permute-start | bytes 294920 | tf_op jit(solution)/shard_map/ppermute | solution.py:508
  97.9 8.0 %collective-permute-start.17 = (f32[1,64,384]{2,1,0:T(8,128)S(1)}, f32[1,64,384]{2,1,0:T(8,128)S(1)}, u32[]{:S(2)}, u32[]{:S(2)}) collective-permute-start(f32[1,64,384]{2,1,0:T(8,128)S(1)} %get-tuple-element.90), channel_id=1, source_target_pairs={{4,0},{8,4},{12,8},{16,12},{20,16},{24,20},{28,24},{0,28},{5,1},{9... | collective-permute-start | bytes 294920 | tf_op jit(solution)/shard_map/ppermute | solution.py:509
  106.0 1.8 %copy-start.11 = (s32[8,128]{1,0:T(8,128)S(1)}, s32[8,128]{1,0:T(8,128)}, u32[]{:S(2)}) copy-start(s32[8,128]{1,0:T(8,128)} %param.20) | copy-start | bytes 12292
  106.0 3.4 %collective-permute-start.18 = (f32[8,8,128]{2,1,0:T(8,128)S(1)}, f32[8,8,128]{2,1,0:T(8,128)S(1)}, u32[]{:S(2)}, u32[]{:S(2)}) collective-permute-start(f32[8,8,128]{2,1,0:T(8,128)S(1)} %get-tuple-element.79), channel_id=1, source_target_pairs={{0,1},{1,2},{2,3},{3,0},{4,5},{5,6},{6,7},{7,4},{8,9},{9,10},{10,1... | collective-permute-start | bytes 98312 | tf_op jit(solution)/shard_map/ppermute | solution.py:508
  106.2 3.2 %collective-permute-start.19 = (f32[8,8,128]{2,1,0:T(8,128)S(1)}, f32[8,8,128]{2,1,0:T(8,128)S(1)}, u32[]{:S(2)}, u32[]{:S(2)}) collective-permute-start(f32[8,8,128]{2,1,0:T(8,128)S(1)} %get-tuple-element.80), channel_id=1, source_target_pairs={{1,0},{2,1},{3,2},{0,3},{5,4},{6,5},{7,6},{4,7},{9,8},{10,9},{11,1... | collective-permute-start | bytes 98312 | tf_op jit(solution)/shard_map/ppermute | solution.py:509
  109.4 12.5 %copy-start.4 = (f32[8,64,384]{2,1,0:T(8,128)S(1)}, f32[8,64,384]{2,1,0:T(8,128)}, u32[]{:S(2)}) copy-start(f32[8,64,384]{2,1,0:T(8,128)} %copy-done.3) | copy-start | bytes 2359300
  128.1 0.7 copy-start.8
where the time goes:
time: 142 us
  Pallas kernels  67 us (47%)
  starting transfers between devices  34.2 us (24%)
  waiting for transfers between devices  26.9 us (19%)
  local copies, waits for them, and re-layouts  11.2 us (8%)
  between operations  1.79 us (1%)
    pallas_call x14, Pallas kernels, local_call(): pl.pallas_call(body, out_shape=[jax.ShapeDtypeStruct(s, F32) for s in out...  35.7 us
    pallas_call x3, Pallas kernels, device_sum(): pl.pallas_call(partial(sum_kernel, wide, narrow, scatter), out_shape=jax....  31.4 us
    ppermute x10, starting transfers between devices, swap(): lax.ppermute(to_prev, axis, [((i + 1) % count, i) for i in range(count)])  28.9 us
    ppermute x10, waiting for transfers between devices, swap(): lax.ppermute(to_next, axis, [(i, (i + 1) % count) for i in range(count)])  20.6 us
    ppermute x10, waiting for transfers between devices, swap(): lax.ppermute(to_prev, axis, [((i + 1) % count, i) for i in range(count)])  6.25 us
    ppermute x10, starting transfers between devices, swap(): lax.ppermute(to_next, axis, [(i, (i + 1) % count) for i in range(count)])  5.29 us
    unnamed x33, local copies, waits for them, and re-layouts  4.3 us
  transfers between devices with their start and end apart: 20, of which 13 were waited for; matrix products, arithmetic and copies ran while one was open for 5% of the time, Pallas kernels for 0%

commit v1 on v0

--- a/solution.py
+++ b/solution.py
@@ -267,6 +267,11 @@
         flat = combine([float(v) for v in LINEAR[a]], planes)
         corners.append(mm(ljk_ref[...], split_rows(flat))[0:4])
     corners = jnp.concatenate(corners, axis=0)
+    stored = []
+    for c in range(3):
+        moved = [mm(p, place) for p in exact_parts(corners[:, 128 * c : 128 * c + 128])]
+        stored.append((moved[0] + moved[1]) + moved[2])
+    corners = jnp.concatenate(stored, axis=1)
     share = AROUND_DEV * (RADIAL + 1)
     ids = ids_ref[...]
     owner = ids // share
@@ -534,9 +539,6 @@
     fdm_values,
 ):
     wide_count, narrow_count = lax.axis_size("wide"), lax.axis_size("narrow")
-    slot_of = element_slot[0]
-    inverse_slot = jnp.zeros((128,), jnp.int32).at[slot_of].set(jnp.arange(128, dtype=jnp.int32))
-    ids = corner_vertex[:, inverse_slot]
     er = jnp.arange(128) % RADIAL
     hz = jnp.broadcast_to(axial_size, (128,))
     ht = jnp.tile(arc_size, AROUND_DEV)
@@ -552,8 +554,9 @@
 
     transform = fdm_vectors.T.reshape(10, 1, 10, 1) * fdm_vectors.T.reshape(1, 10, 1, 10)
     own = transform[..., 1:9].reshape(100, 80)
-    halo = jnp.zeros((10, 10, 10, 8), F32)
-    halo = halo.at[..., 6].set(transform[..., 0]).at[..., 1].set(transform[..., 9])
+    blank = jnp.zeros((10, 10, 10), F32)
+    halo = [blank, transform[..., 9]] + [blank] * 4 + [transform[..., 0], blank]
+    halo = jnp.stack(halo, axis=-1)
     into = jnp.pad(jnp.concatenate([own, halo.reshape(100, 80)], axis=1), ((0, 12), (0, 0)))
     inner = fdm_vectors[1:9]
     outof = (inner.reshape(8, 1, 10, 1) * inner.reshape(1, 8, 1, 10)).reshape(64, 100)
@@ -586,7 +589,7 @@
     share = AROUND_DEV * (RADIAL + 1)
     out, full = local_call(
         partial(leave_kernel, owners),
-        (u.reshape(512, 384), res.reshape(512, 384), element_slot, ids, jnp.asarray(LINEAR_JK)),
+        (u.reshape(512, 384), res.reshape(512, 384), element_slot, corner_vertex, jnp.asarray(LINEAR_JK)),
         [(3, 512, 128), (3 * owners, 256)],
         [],
     )

time: 142 us -> 143 us (level)
    unnamed x33 -> x32, local copies, waits for them, and re-layouts: 4.3 us -> 7.43 us
    ppermute x10, waiting for transfers between devices: 6.25 us -> 3.65 us  [swap(): lax.ppermute(to_prev, axis, [((i + 1) % count, i) for i in range(count)])]
    scatter x3 -> x0, local copies, waits for them, and re-layouts: 2.52 us -> none  [the longest x2 1.55 us: shards(): halo.at[..., 6].set(transform[..., 0]).at[..., 1].set(transform[..., 9])]
    ppermute x10, waiting for transfers between devices: 20.6 us -> 22.2 us  [swap(): lax.ppermute(to_next, axis, [(i, (i + 1) % count) for i in range(count)])]
  transfers between devices with their start and end apart: 20 -> 20, of which waited for: 13 -> 12; matrix products, arithmetic and copies ran while one was open for 5% -> 4% of each run, Pallas kernels for 0% -> 0%
where the time goes in v1:
time: 143 us; the launch traced here: 142 us
  Pallas kernels  68.4 us (48%)
  starting transfers between devices  34.2 us (24%)
  waiting for transfers between devices  25.9 us (18%)
  local copies, waits for them, and re-layouts  11.7 us (8%)
  between operations  1.75 us (1%)
    pallas_call x14, Pallas kernels, local_call(): pl.pallas_call(body, out_shape=[jax.ShapeDtypeStruct(s, F32) for s in out...  35.7 us
    pallas_call x3, Pallas kernels, device_sum(): pl.pallas_call(partial(sum_kernel, wide, narrow, scatter), out_shape=jax....  32.7 us
    ppermute x10, starting transfers between devices, swap(): lax.ppermute(to_prev, axis, [((i + 1) % count, i) for i in range(count)])  28.1 us
    ppermute x10, waiting for transfers between devices, swap(): lax.ppermute(to_next, axis, [(i, (i + 1) % count) for i in range(count)])  22.2 us
    unnamed x32, local copies, waits for them, and re-layouts  7.43 us
    ppermute x10, starting transfers between devices, swap(): lax.ppermute(to_next, axis, [(i, (i + 1) % count) for i in range(count)])  6.04 us
    ppermute x10, waiting for transfers between devices, swap(): lax.ppermute(to_prev, axis, [((i + 1) % count, i) for i in range(count)])  3.65 us
  transfers between devices with their start and end apart: 20, of which 12 were waited for; matrix products, arithmetic and copies ran while one was open for 4% of the time, Pallas kernels for 0%

profile of v1, /device:TPU:0, one launch (start us, length us, event | category | flops | bytes accessed | tf_op | source)
XLA Modules:
  0.0 142.4 jit_solution(4883578610369198041)
XLA Ops:
  1.3 0.6 copy-done.12
  2.1 0.6 copy-done.10
  2.6 0.1 broadcast_multiply_fusion.2.mass_ref
  2.8 0.5 copy-done.8
  3.3 1.1 copy-done.2
  4.4 0.5 shard_map.149
  5.0 3.0 %collective-permute-start = (f32[1,64,512]{2,1,0:T(8,128)S(1)}, f32[1,64,512]{2,1,0:T(8,128)S(1)}, u32[]{:S(2)}, u32[]{:S(2)}) collective-permute-start(f32[1,64,512]{2,1,0:T(8,128)S(1)} %get-tuple-element.65), channel_id=1, source_target_pairs={{0,4},{4,8},{8,12},{12,16},{16,20},{20,24},{24,28},{28,0},{1,5},{5... | collective-permute-start | bytes 393224 | tf_op jit(solution)/shard_map/ppermute | solution.py:513
  8.0 3.1 %collective-permute-start.1 = (f32[1,64,512]{2,1,0:T(8,128)S(1)}, f32[1,64,512]{2,1,0:T(8,128)S(1)}, u32[]{:S(2)}, u32[]{:S(2)}) collective-permute-start(f32[1,64,512]{2,1,0:T(8,128)S(1)} %get-tuple-element.64), channel_id=1, source_target_pairs={{4,0},{8,4},{12,8},{16,12},{20,16},{24,20},{28,24},{0,28},{5,1},{9... | collective-permute-start | bytes 393224 | tf_op jit(solution)/shard_map/ppermute | solution.py:514
  11.2 0.6 broadcast_dynamic-update-slice_fusion.1
  12.0 0.5 copy-done.4
  12.6 0.7 slice_dynamic-update-slice_fusion.1
  13.3 0.8 broadcast_dynamic-update-slice_fusion
  14.1 0.6 slice_dynamic-update-slice_fusion
  14.7 0.6 broadcast_dynamic-update-slice_fusion.2
  15.4 1.3 reshape.140
  16.8 0.2 reshape.139
  17.2 0.1 shard_map.150
  17.4 1.7 %collective-permute-start.3 = (f32[8,8,128]{2,1,0:T(8,128)S(1)}, f32[8,8,128]{2,1,0:T(8,128)S(1)}, u32[]{:S(2)}, u32[]{:S(2)}) collective-permute-start(f32[8,8,128]{2,1,0:T(8,128)S(1)} %get-tuple-element.35), channel_id=1, source_target_pairs={{1,0},{2,1},{3,2},{0,3},{5,4},{6,5},{7,6},{4,7},{9,8},{10,9},{11,1... | collective-permute-start | bytes 98312 | tf_op jit(solution)/shard_map/ppermute | solution.py:514
  19.4 0.6 copy-done.5
  20.2 0.6 collective-permute-done.2.prev_ref
  20.9 6.9 %shard_map.151 = (f32[8,64,384]{2,1,0:T(8,128)S(1)}, f32[8,64,384]{2,1,0:T(8,128)S(1)}) custom-call(f32[8,64,512]{2,1,0:T(8,128)S(1)} %get-tuple-element.33.y_ref, f32[8,8,128]{2,1,0:T(8,128)S(1)} %collective-permute-done.2.prev_ref, f32[8,8,128]{2,1,0:T(8,128)S(1)} %collective-permute-done.3.next_ref, f32[8,384]{1,0:T(8,128)S(1)} %broadcast_bitcast_fusion.geo_ref, ...), custom_call_target="tpu_custom_call" | custom-call | tf_op jit(solution)/shard_map/pallas_call | solution.py:498
  27.9 4.7 %collective-permute-start.5 = (f32[2,64,384]{2,1,0:T(8,128)S(1)}, f32[2,64,384]{2,1,0:T(8,128)S(1)}, u32[]{:S(2)}, u32[]{:S(2)}) collective-permute-start(f32[2,64,384]{2,1,0:T(8,128)S(1)} %get-tuple-element.72), channel_id=1, source_target_pairs={{4,0},{8,4},{12,8},{16,12},{20,16},{24,20},{28,24},{0,28},{5,1},{9... | collective-permute-start | bytes 589832 | tf_op jit(solution)/shard_map/ppermute | solution.py:514
  32.7 5.1 %collective-permute-done.4.below_ref = f32[2,64,384]{2,1,0:T(8,128)S(1)} collective-permute-done((f32[2,64,384]{2,1,0:T(8,128)S(1)}, f32[2,64,384]{2,1,0:T(8,128)S(1)}, u32[]{:S(2)}, u32[]{:S(2)}) %collective-permute-start.4) | collective-permute-done | bytes 196640 | tf_op jit(solution)/shard_map/ppermute | solution.py:513
  37.8 1.5 %collective-permute-done.5.above_ref = f32[2,64,384]{2,1,0:T(8,128)S(1)} collective-permute-done((f32[2,64,384]{2,1,0:T(8,128)S(1)}, f32[2,64,384]{2,1,0:T(8,128)S(1)}, u32[]{:S(2)}, u32[]{:S(2)}) %collective-permute-start.5) | collective-permute-done | bytes 196640 | tf_op jit(solution)/shard_map/ppermute | solution.py:514
  39.3 0.2 shard_map.152
  39.5 0.6 collective-permute-start.6
  40.0 1.2 collective-permute-start.7
  41.3 0.2 mul.87
  41.6 0.1 copy.33
  41.7 1.3 collective-permute-done.6.prev_ref
  43.0 5.0 %shard_map.153 = (f32[8,64,384]{2,1,0:T(8,128)S(1)}, f32[8,64,384]{2,1,0:T(8,128)S(1)}) custom-call(f32[10,64,384]{2,1,0:T(8,128)S(1)} %get-tuple-element.38.y_ref, f32[10,8,128]{2,1,0:T(8,128)S(1)} %collective-permute-done.6.prev_ref, f32[10,8,128]{2,1,0:T(8,128)S(1)} %collective-permute-done.7.next_ref, f32[8,384]{1,0:T(8,128)S(1)} %broadcast_bitcast_fusion.geo_ref, ...), custom_call_target="tpu_custom_call" | custom-call | tf_op jit(solution)/shard_map/pallas_call | solution.py:498
  48.0 0.2 collective-permute-start.8
  48.2 4.6 %collective-permute-start.9 = (f32[1,64,384]{2,1,0:T(8,128)S(1)}, f32[1,64,384]{2,1,0:T(8,128)S(1)}, u32[]{:S(2)}, u32[]{:S(2)}) collective-permute-start(f32[1,64,384]{2,1,0:T(8,128)S(1)} %get-tuple-element.70), channel_id=1, source_target_pairs={{4,0},{8,4},{12,8},{16,12},{20,16},{24,20},{28,24},{0,28},{5,1},{9... | collective-permute-start | bytes 294920 | tf_op jit(solution)/shard_map/ppermute | solution.py:514
  52.8 2.7 %collective-permute-done.8.below_ref = f32[1,64,384]{2,1,0:T(8,128)S(1)} collective-permute-done((f32[1,64,384]{2,1,0:T(8,128)S(1)}, f32[1,64,384]{2,1,0:T(8,128)S(1)}, u32[]{:S(2)}, u32[]{:S(2)}) %collective-permute-start.8) | collective-permute-done | bytes 98336 | tf_op jit(solution)/shard_map/ppermute | solution.py:513
  55.5 0.1 shard_map.154
  55.7 1.0 collective-permute-start.10
  56.6 0.8 collective-permute-start.11
  57.5 1.6 %collective-permute-done.10.prev_ref = f32[8,8,128]{2,1,0:T(8,128)S(1)} collective-permute-done((f32[8,8,128]{2,1,0:T(8,128)S(1)}, f32[8,8,128]{2,1,0:T(8,128)S(1)}, u32[]{:S(2)}, u32[]{:S(2)}) %collective-permute-start.10) | collective-permute-done | bytes 32800 | tf_op jit(solution)/shard_map/ppermute | solution.py:513
  59.1 0.1 collective-permute-done.11.next_ref
  59.2 1.6 %shard_map.155 = (f32[8,64,384]{2,1,0:T(8,128)S(1)}, f32[8,128]{1,0:T(8,128)S(1)}) custom-call(f32[8,64,384]{2,1,0:T(8,128)S(1)} %get-tuple-element.42.y_ref, f32[8,8,128]{2,1,0:T(8,128)S(1)} %collective-permute-done.10.prev_ref, f32[8,8,128]{2,1,0:T(8,128)S(1)} %collective-permute-done.11.next_ref, f32[8,64,384]{2,1,0:T(8,128)S(1)} %get-tuple-element.45.res_ref, ...), custom_call_target="tpu_custom_call" | custom-call | tf_op jit(solution)/shard_map/pallas_call | solution.py:498
  60.8 11.5 %shard_map.156.sums_ref = f32[8,128]{1,0:T(8,128)S(1)} custom-call(f32[8,128]{1,0:T(8,128)S(1)} %get-tuple-element.47.x_ref), custom_call_target="tpu_custom_call" | custom-call | tf_op jit(solution)/shard_map/pallas_call | solution.py:477
  72.3 6.2 %shard_map.157 = (f32[8,64,384]{2,1,0:T(8,128)S(1)}, f32[8,64,384]{2,1,0:T(8,128)S(1)}) custom-call(f32[8,64,384]{2,1,0:T(8,128)S(1)} %get-tuple-element.36.u_in, f32[8,64,384]{2,1,0:T(8,128)S(1)} %get-tuple-element.46.dirn_ref, f32[8,128]{1,0:T(8,128)S(1)} %shard_map.156.sums_ref, f32[8,384]{1,0:T(8,128)S(1)} %broadcast_bitcast_fusion.geo_ref, ...), custom_call_target="tpu_custom_call" | custom-call | tf_op jit(solution)/shard_map/pallas_call | solution.py:498
  78.6 0.6 collective-permute-start.12
  79.2 4.1 %collective-permute-start.13 = (f32[2,64,384]{2,1,0:T(8,128)S(1)}, f32[2,64,384]{2,1,0:T(8,128)S(1)}, u32[]{:S(2)}, u32[]{:S(2)}) collective-permute-start(f32[2,64,384]{2,1,0:T(8,128)S(1)} %get-tuple-element.68), channel_id=1, source_target_pairs={{4,0},{8,4},{12,8},{16,12},{20,16},{24,20},{28,24},{0,28},{5,1},{9... | collective-permute-start | bytes 589832 | tf_op jit(solution)/shard_map/ppermute | solution.py:514
  83.3 4.1 %collective-permute-done.12.below_ref = f32[2,64,384]{2,1,0:T(8,128)S(1)} collective-permute-done((f32[2,64,384]{2,1,0:T(8,128)S(1)}, f32[2,64,384]{2,1,0:T(8,128)S(1)}, u32[]{:S(2)}, u32[]{:S(2)}) %collective-permute-start.12) | collective-permute-done | bytes 196640 | tf_op jit(solution)/shard_map/ppermute | solution.py:513
  87.5 2.0 %collective-permute-done.13.above_ref = f32[2,64,384]{2,1,0:T(8,128)S(1)} collective-permute-done((f32[2,64,384]{2,1,0:T(8,128)S(1)}, f32[2,64,384]{2,1,0:T(8,128)S(1)}, u32[]{:S(2)}, u32[]{:S(2)}) %collective-permute-start.13) | collective-permute-done | bytes 196640 | tf_op jit(solution)/shard_map/ppermute | solution.py:514
  89.5 0.2 shard_map.158
  89.7 1.7 %collective-permute-start.15 = (f32[10,8,128]{2,1,0:T(8,128)S(1)}, f32[10,8,128]{2,1,0:T(8,128)S(1)}, u32[]{:S(2)}, u32[]{:S(2)}) collective-permute-start(f32[10,8,128]{2,1,0:T(8,128)S(1)} %get-tuple-element.52), channel_id=1, source_target_pairs={{1,0},{2,1},{3,2},{0,3},{5,4},{6,5},{7,6},{4,7},{9,8},{10,9},{11,1... | collective-permute-start | bytes 122888 | tf_op jit(solution)/shard_map/ppermute | solution.py:514
  91.5 1.7 %collective-permute-done.14.prev_ref = f32[10,8,128]{2,1,0:T(8,128)S(1)} collective-permute-done((f32[10,8,128]{2,1,0:T(8,128)S(1)}, f32[10,8,128]{2,1,0:T(8,128)S(1)}, u32[]{:S(2)}, u32[]{:S(2)}) %collective-permute-start.14) | collective-permute-done | bytes 40992 | tf_op jit(solution)/shard_map/ppermute | solution.py:513
  93.2 5.0 %shard_map.159 = (f32[8,64,384]{2,1,0:T(8,128)S(1)}, f32[8,64,384]{2,1,0:T(8,128)S(1)}) custom-call(f32[10,64,384]{2,1,0:T(8,128)S(1)} %get-tuple-element.50.y_ref, f32[10,8,128]{2,1,0:T(8,128)S(1)} %collective-permute-done.14.prev_ref, f32[10,8,128]{2,1,0:T(8,128)S(1)} %collective-permute-done.15.next_ref, f32[8,384]{1,0:T(8,128)S(1)} %broadcast_bitcast_fusion.geo_ref, ...), custom_call_target="tpu_custom_call" | custom-call | tf_op jit(solution)/shard_map/pallas_call | solution.py:498
  98.2 0.3 collective-permute-start.16
  98.6 4.4 %collective-permute-start.17 = (f32[1,64,384]{2,1,0:T(8,128)S(1)}, f32[1,64,384]{2,1,0:T(8,128)S(1)}, u32[]{:S(2)}, u32[]{:S(2)}) collective-permute-start(f32[1,64,384]{2,1,0:T(8,128)S(1)} %get-tuple-element.66), channel_id=1, source_target_pairs={{4,0},{8,4},{12,8},{16,12},{20,16},{24,20},{28,24},{0,28},{5,1},{9... | collective-permute-start | bytes 294920 | tf_op jit(solution)/shard_map/ppermute | solution.py:514
  103.0 3.6 %collective-permute-done.16.below_ref = f32[1,64,384]{2,1,0:T(8,128)S(1)} collective-permute-done((f32[1,64,384]{2,1,0:T(8,128)S(1)}, f32[1,64,384]{2,1,0:T(8,128)S(1)}, u32[]{:S(2)}, u32[]{:S(2)}) %collective-permute-start.16) | collective-permute-done | bytes 98336 | tf_op jit(solution)/shard_map/ppermute | solution.py:513
  106.6 0.1 shard_map.160
  106.7 0.2 collective-permute-start.18
  106.9 1.6 %collective-permute-start.19 = (f32[8,8,128]{2,1,0:T(8,128)S(1)}, f32[8,8,128]{2,1,0:T(8,128)S(1)}, u32[]{:S(2)}, u32[]{:S(2)}) collective-permute-start(f32[8,8,128]{2,1,0:T(8,128)S(1)} %get-tuple-element.56), channel_id=1, source_target_pairs={{1,0},{2,1},{3,2},{0,3},{5,4},{6,5},{7,6},{4,7},{9,8},{10,9},{11,1... | collective-permute-start | bytes 98312 | tf_op jit(solution)/shard_map/ppermute | solution.py:514
  108.5 1.6 %collective-permute-done.18.prev_ref = f32[8,8,128]{2,1,0:T(8,128)S(1)} collective-permute-done((f32[8,8,128]{2,1,0:T(8,128)S(1)}, f32[8,8,128]{2,1,0:T(8,128)S(1)}, u32[]{:S(2)}, u32[]{:S(2)}) %collective-permute-start.18) | collective-permute-done | bytes 32800 | tf_op jit(solution)/shard_map/ppermute | solution.py:513
  110.1 1.6 %shard_map.161 = (f32[8,64,384]{2,1,0:T(8,128)S(1)}, f32[8,128]{1,0:T(8,128)S(1)}) custom-call(f32[8,64,384]{2,1,0:T(8,128)S(1)} %get-tuple-element.54.y_ref, f32[8,8,128]{2,1,0:T(8,128)S(1)} %collective-permute-done.18.prev_ref, f32[8,8,128]{2,1,0:T(8,128)S(1)} %collective-permute-done.19.next_ref, f32[8,64,384]{2,1,0:T(8,128)S(1)} %get-tuple-element.57.res_ref, ...), custom_call_target="tpu_custom_call" | custom-call | tf_op jit(solution)/shard_map/pallas_call | solution.py:498
  111.7 10.8 %shard_map.162.sums_ref = f32[8,128]{1,0:T(8,128)S(1)} custom-call(f32[8,128]{1,0:T(8,128)S(1)} %get-tuple-element.59.x_ref), custom_call_target="tpu_custom_call" | custom-call | tf_op jit(solution)/shard_map/pallas_call | solution.py:477
  122.5 6.2 %shard_map.163 = (f32[8,64,384]{2,1,0:T(8,128)S(1)}, f32[8,64,384]{2,1,0:T(8,128)S(1)}) custom-call(f32[8,64,384]{2,1,0:T(8,128)S(1)} %get-tuple-element.48.u_in, f32[8,64,384]{2,1,0:T(8,128)S(1)} %get-tuple-element.58.dirn_ref, f32[8,128]{1,0:T(8,128)S(1)} %shard_map.162.sums_ref, f32[8,384]{1,0:T(8,128)S(1)} %broadcast_bitcast_fusion.geo_ref, ...), custom_call_target="tpu_custom_call" | custom-call | tf_op jit(solution)/shard_map/pallas_call | solution.py:498
  128.7 0.7 copy-done.6
  129.4 1.8 %shard_map.164 = (f32[3,512,128]{2,1,0:T(8,128)}, f32[96,256]{1,0:T(8,128)S(1)}) custom-call(f32[512,384]{1,0:T(8,128)S(1)} %bitcast.25, f32[512,384]{1,0:T(8,128)S(1)} %bitcast.26, s32[1,128]{1,0:T(1,128)S(1)} %copy-done.8, s32[8,128]{1,0:T(8,128)S(1)} %copy-done.6, bf16[8,192]{1,0:T(8,128)(2,1)S(1)} %copy-done.7), custom_call_target="tpu_custom_call" | custom-call | tf_op jit(solution)/shard_map/pallas_call | solution.py:498
  131.4 10.4 %shard_map.165 = f32[8,256]{1,0:T(8,128)S(1)} custom-call(f32[4,8,8,256]{3,2,1,0:T(8,128)S(1)} %pad.19.x_ref), custom_call_target="tpu_custom_call" | custom-call | tf_op jit(solution)/shard_map/pallas_call | solution.py:477
  141.8 0.6 slice.67
  (71 shorter events, 1.9 us)
Async XLA Ops:
  1.3 0.7 copy-start.12
  1.3 0.7 copy-start.13
  2.0 0.7 copy-start.10
  2.6 0.7 copy-start.8
  3.3 1.1 copy-start.2
  5.0 12.2 %collective-permute-start = (f32[1,64,512]{2,1,0:T(8,128)S(1)}, f32[1,64,512]{2,1,0:T(8,128)S(1)}, u32[]{:S(2)}, u32[]{:S(2)}) collective-permute-start(f32[1,64,512]{2,1,0:T(8,128)S(1)} %get-tuple-element.65), channel_id=1, source_target_pairs={{0,4},{4,8},{8,12},{12,16},{16,20},{20,24},{24,28},{28,0},{1,5},{5... | collective-permute-start | bytes 393224 | tf_op jit(solution)/shard_map/ppermute | solution.py:513
  8.0 9.2 %collective-permute-start.1 = (f32[1,64,512]{2,1,0:T(8,128)S(1)}, f32[1,64,512]{2,1,0:T(8,128)S(1)}, u32[]{:S(2)}, u32[]{:S(2)}) collective-permute-start(f32[1,64,512]{2,1,0:T(8,128)S(1)} %get-tuple-element.64), channel_id=1, source_target_pairs={{4,0},{8,4},{12,8},{16,12},{20,16},{24,20},{28,24},{0,28},{5,1},{9... | collective-permute-start | bytes 393224 | tf_op jit(solution)/shard_map/ppermute | solution.py:514
  11.8 0.7 copy-start.4
  12.6 1.4 %copy-start.9 = (f32[10,10,10,10]{1,0,3,2:T(8,128)}, f32[10,10,10,10]{1,0,3,2:T(8,128)S(1)}, u32[]{:S(2)}) copy-start(f32[10,10,10,10]{1,0,3,2:T(8,128)S(1)} %broadcast_multiply_fusion) | copy-start | bytes 120004
  14.7 2.0 %slice-start = ((f32[10,10,10,10]{1,0,3,2:T(8,128)}), f32[10,10,10,8]{1,0,3,2:T(8,128)S(1)}, s32[]{:S(2)}) async-start(f32[10,10,10,10]{1,0,3,2:T(8,128)} %copy-done.9), calls=%async_computation | async-start | bytes 1310720 | tf_op jit(solution)/shard_map/slice | solution.py:556
  17.4 3.5 %copy-start = (bf16[432,192]{1,0:T(8,128)(2,1)S(1)}, bf16[432,192]{1,0:T(8,128)(2,1)}, u32[]{:S(2)}) copy-start(bf16[432,192]{1,0:T(8,128)(2,1)} %constant.44.clone.fwd) | copy-start | bytes 497668
  17.4 3.4 %collective-permute-start.2 = (f32[8,8,128]{2,1,0:T(8,128)S(1)}, f32[8,8,128]{2,1,0:T(8,128)S(1)}, u32[]{:S(2)}, u32[]{:S(2)}) collective-permute-start(f32[8,8,128]{2,1,0:T(8,128)S(1)} %get-tuple-element.34), channel_id=1, source_target_pairs={{0,1},{1,2},{2,3},{3,0},{4,5},{5,6},{6,7},{7,4},{8,9},{9,10},{10,1... | collective-permute-start | bytes 98312 | tf_op jit(solution)/shard_map/ppermute | solution.py:513
  17.4 3.3 %collective-permute-start.3 = (f32[8,8,128]{2,1,0:T(8,128)S(1)}, f32[8,8,128]{2,1,0:T(8,128)S(1)}, u32[]{:S(2)}, u32[]{:S(2)}) collective-permute-start(f32[8,8,128]{2,1,0:T(8,128)S(1)} %get-tuple-element.35), channel_id=1, source_target_pairs={{1,0},{2,1},{3,2},{0,3},{5,4},{6,5},{7,6},{4,7},{9,8},{10,9},{11,1... | collective-permute-start | bytes 98312 | tf_op jit(solution)/shard_map/ppermute | solution.py:514
  19.2 1.6 %copy-start.11 = (f32[64]{0:T(128)S(1)}, f32[64]{0:T(128)}, u32[]{:S(2)}) copy-start(f32[64]{0:T(128)} %constant.47.clone) | copy-start | bytes 772
  19.3 0.7 copy-start.5
  19.9 0.9 copy-start.3
  19.9 0.9 copy-start.1
  27.9 9.9 %collective-permute-start.4 = (f32[2,64,384]{2,1,0:T(8,128)S(1)}, f32[2,64,384]{2,1,0:T(8,128)S(1)}, u32[]{:S(2)}, u32[]{:S(2)}) collective-permute-start(f32[2,64,384]{2,1,0:T(8,128)S(1)} %get-tuple-element.73), channel_id=1, source_target_pairs={{0,4},{4,8},{8,12},{12,16},{16,20},{20,24},{24,28},{28,0},{1,5},{5... | collective-permute-start | bytes 589832 | tf_op jit(solution)/shard_map/ppermute | solution.py:513
  27.9 11.3 %collective-permute-start.5 = (f32[2,64,384]{2,1,0:T(8,128)S(1)}, f32[2,64,384]{2,1,0:T(8,128)S(1)}, u32[]{:S(2)}, u32[]{:S(2)}) collective-permute-start(f32[2,64,384]{2,1,0:T(8,128)S(1)} %get-tuple-element.72), channel_id=1, source_target_pairs={{4,0},{8,4},{12,8},{16,12},{20,16},{24,20},{28,24},{0,28},{5,1},{9... | collective-permute-start | bytes 589832 | tf_op jit(solution)/shard_map/ppermute | solution.py:514
  39.5 3.5 %collective-permute-start.6 = (f32[10,8,128]{2,1,0:T(8,128)S(1)}, f32[10,8,128]{2,1,0:T(8,128)S(1)}, u32[]{:S(2)}, u32[]{:S(2)}) collective-permute-start(f32[10,8,128]{2,1,0:T(8,128)S(1)} %get-tuple-element.39), channel_id=1, source_target_pairs={{0,1},{1,2},{2,3},{3,0},{4,5},{5,6},{6,7},{7,4},{8,9},{9,10},{10,1... | collective-permute-start | bytes 122888 | tf_op jit(solution)/shard_map/ppermute | solution.py:513
  40.0 2.9 %collective-permute-start.7 = (f32[10,8,128]{2,1,0:T(8,128)S(1)}, f32[10,8,128]{2,1,0:T(8,128)S(1)}, u32[]{:S(2)}, u32[]{:S(2)}) collective-permute-start(f32[10,8,128]{2,1,0:T(8,128)S(1)} %get-tuple-element.40), channel_id=1, source_target_pairs={{1,0},{2,1},{3,2},{0,3},{5,4},{6,5},{7,6},{4,7},{9,8},{10,9},{11,1... | collective-permute-start | bytes 122888 | tf_op jit(solution)/shard_map/ppermute | solution.py:514
  48.0 7.5 %collective-permute-start.8 = (f32[1,64,384]{2,1,0:T(8,128)S(1)}, f32[1,64,384]{2,1,0:T(8,128)S(1)}, u32[]{:S(2)}, u32[]{:S(2)}) collective-permute-start(f32[1,64,384]{2,1,0:T(8,128)S(1)} %get-tuple-element.71), channel_id=1, source_target_pairs={{0,4},{4,8},{8,12},{12,16},{16,20},{20,24},{24,28},{28,0},{1,5},{5... | collective-permute-start | bytes 294920 | tf_op jit(solution)/shard_map/ppermute | solution.py:513
  48.2 7.3 %collective-permute-start.9 = (f32[1,64,384]{2,1,0:T(8,128)S(1)}, f32[1,64,384]{2,1,0:T(8,128)S(1)}, u32[]{:S(2)}, u32[]{:S(2)}) collective-permute-start(f32[1,64,384]{2,1,0:T(8,128)S(1)} %get-tuple-element.70), channel_id=1, source_target_pairs={{4,0},{8,4},{12,8},{16,12},{20,16},{24,20},{28,24},{0,28},{5,1},{9... | collective-permute-start | bytes 294920 | tf_op jit(solution)/shard_map/ppermute | solution.py:514
  55.7 3.4 %collective-permute-start.10 = (f32[8,8,128]{2,1,0:T(8,128)S(1)}, f32[8,8,128]{2,1,0:T(8,128)S(1)}, u32[]{:S(2)}, u32[]{:S(2)}) collective-permute-start(f32[8,8,128]{2,1,0:T(8,128)S(1)} %get-tuple-element.43), channel_id=1, source_target_pairs={{0,1},{1,2},{2,3},{3,0},{4,5},{5,6},{6,7},{7,4},{8,9},{9,10},{10,1... | collective-permute-start | bytes 98312 | tf_op jit(solution)/shard_map/ppermute | solution.py:513
  56.6 2.6 %collective-permute-start.11 = (f32[8,8,128]{2,1,0:T(8,128)S(1)}, f32[8,8,128]{2,1,0:T(8,128)S(1)}, u32[]{:S(2)}, u32[]{:S(2)}) collective-permute-start(f32[8,8,128]{2,1,0:T(8,128)S(1)} %get-tuple-element.44), channel_id=1, source_target_pairs={{1,0},{2,1},{3,2},{0,3},{5,4},{6,5},{7,6},{4,7},{9,8},{10,9},{11,1... | collective-permute-start | bytes 98312 | tf_op jit(solution)/shard_map/ppermute | solution.py:514
  78.6 8.9 %collective-permute-start.12 = (f32[2,64,384]{2,1,0:T(8,128)S(1)}, f32[2,64,384]{2,1,0:T(8,128)S(1)}, u32[]{:S(2)}, u32[]{:S(2)}) collective-permute-start(f32[2,64,384]{2,1,0:T(8,128)S(1)} %get-tuple-element.69), channel_id=1, source_target_pairs={{0,4},{4,8},{8,12},{12,16},{16,20},{20,24},{24,28},{28,0},{1,5},{5... | collective-permute-start | bytes 589832 | tf_op jit(solution)/shard_map/ppermute | solution.py:513
  79.2 10.3 %collective-permute-start.13 = (f32[2,64,384]{2,1,0:T(8,128)S(1)}, f32[2,64,384]{2,1,0:T(8,128)S(1)}, u32[]{:S(2)}, u32[]{:S(2)}) collective-permute-start(f32[2,64,384]{2,1,0:T(8,128)S(1)} %get-tuple-element.68), channel_id=1, source_target_pairs={{4,0},{8,4},{12,8},{16,12},{20,16},{24,20},{28,24},{0,28},{5,1},{9... | collective-permute-start | bytes 589832 | tf_op jit(solution)/shard_map/ppermute | solution.py:514
  89.7 3.5 %collective-permute-start.14 = (f32[10,8,128]{2,1,0:T(8,128)S(1)}, f32[10,8,128]{2,1,0:T(8,128)S(1)}, u32[]{:S(2)}, u32[]{:S(2)}) collective-permute-start(f32[10,8,128]{2,1,0:T(8,128)S(1)} %get-tuple-element.51), channel_id=1, source_target_pairs={{0,1},{1,2},{2,3},{3,0},{4,5},{5,6},{6,7},{7,4},{8,9},{9,10},{10,1... | collective-permute-start | bytes 122888 | tf_op jit(solution)/shard_map/ppermute | solution.py:513
  89.7 3.4 %collective-permute-start.15 = (f32[10,8,128]{2,1,0:T(8,128)S(1)}, f32[10,8,128]{2,1,0:T(8,128)S(1)}, u32[]{:S(2)}, u32[]{:S(2)}) collective-permute-start(f32[10,8,128]{2,1,0:T(8,128)S(1)} %get-tuple-element.52), channel_id=1, source_target_pairs={{1,0},{2,1},{3,2},{0,3},{5,4},{6,5},{7,6},{4,7},{9,8},{10,9},{11,1... | collective-permute-start | bytes 122888 | tf_op jit(solution)/shard_map/ppermute | solution.py:514
  98.2 8.3 %collective-permute-start.16 = (f32[1,64,384]{2,1,0:T(8,128)S(1)}, f32[1,64,384]{2,1,0:T(8,128)S(1)}, u32[]{:S(2)}, u32[]{:S(2)}) collective-permute-start(f32[1,64,384]{2,1,0:T(8,128)S(1)} %get-tuple-element.67), channel_id=1, source_target_pairs={{0,4},{4,8},{8,12},{12,16},{16,20},{20,24},{24,28},{28,0},{1,5},{5... | collective-permute-start | bytes 294920 | tf_op jit(solution)/shard_map/ppermute | solution.py:513
  98.6 8.0 %collective-permute-start.17 = (f32[1,64,384]{2,1,0:T(8,128)S(1)}, f32[1,64,384]{2,1,0:T(8,128)S(1)}, u32[]{:S(2)}, u32[]{:S(2)}) collective-permute-start(f32[1,64,384]{2,1,0:T(8,128)S(1)} %get-tuple-element.66), channel_id=1, source_target_pairs={{4,0},{8,4},{12,8},{16,12},{20,16},{24,20},{28,24},{0,28},{5,1},{9... | collective-permute-start | bytes 294920 | tf_op jit(solution)/shard_map/ppermute | solution.py:514
  106.7 3.4 %collective-permute-start.18 = (f32[8,8,128]{2,1,0:T(8,128)S(1)}, f32[8,8,128]{2,1,0:T(8,128)S(1)}, u32[]{:S(2)}, u32[]{:S(2)}) collective-permute-start(f32[8,8,128]{2,1,0:T(8,128)S(1)} %get-tuple-element.55), channel_id=1, source_target_pairs={{0,1},{1,2},{2,3},{3,0},{4,5},{5,6},{6,7},{7,4},{8,9},{9,10},{10,1... | collective-permute-start | bytes 98312 | tf_op jit(solution)/shard_map/ppermute | solution.py:513
  106.9 3.2 %collective-permute-start.19 = (f32[8,8,128]{2,1,0:T(8,128)S(1)}, f32[8,8,128]{2,1,0:T(8,128)S(1)}, u32[]{:S(2)}, u32[]{:S(2)}) collective-permute-start(f32[8,8,128]{2,1,0:T(8,128)S(1)} %get-tuple-element.56), channel_id=1, source_target_pairs={{1,0},{2,1},{3,2},{0,3},{5,4},{6,5},{7,6},{4,7},{9,8},{10,9},{11,1... | collective-permute-start | bytes 98312 | tf_op jit(solution)/shard_map/ppermute | solution.py:514
  122.5 6.2 %copy-start.7 = (bf16[8,192]{1,0:T(8,128)(2,1)S(1)}, bf16[8,192]{1,0:T(8,128)(2,1)}, u32[]{:S(2)}) copy-start(bf16[8,192]{1,0:T(8,128)(2,1)} %constant.49.clone.ljk_ref) | copy-start | bytes 9220
  128.7 0.7 copy-start.6
